TPU v7x, 512 devices: a whole 4x8x8 slice. The times are simulated.
512 devices in a mesh: inst: 64 (over y, x, core), tp: 8 (over z).
Axes of the slice: x: 4, y: 8, z: 8, core: 2. Of those that a mesh axis runs over, the one named last changes fastest.
Arguments:
- query: bfloat16 [4096, 64, 128], P('inst', 'tp'), may hold values from -8 to 8
- key_cache: bfloat16 [16384, 8, 128], P('inst', 'tp'), may hold values from -8 to 8
- value_cache: bfloat16 [16384, 8, 128], P('inst', 'tp'), may hold values from -6 to 6
- span_keys: bfloat16 [4096, 8, 128], P('inst', 'tp'), may hold values from -8 to 8
- span_values: bfloat16 [4096, 8, 128], P('inst', 'tp'), may hold values from -6 to 6
- live_pages: int32 [64], P('inst'), may hold values from 24 to 32
- routes: int32 [2048, 1], P('inst'), may hold values from 0 to 63; in each aligned block of 32 rows (0 to 31, 32 to 63, ...) no two rows name the same one
- decode_query: bfloat16 [64, 128], P('tp'), may hold values from -8 to 8
- new_key: bfloat16 [8, 128], P('tp'), may hold values from -8 to 8
- new_value: bfloat16 [8, 128], P('tp'), may hold values from -6 to 6
- w_out: bfloat16 [8192, 8192], P('tp', 'inst'), may hold values from -0.0625 to 0.0625
Outputs:
- span_out: bfloat16 [4096, 64, 128], P('inst', 'tp')
- held_keys: bfloat16 [4096, 8, 8, 128], P('inst', None, 'tp')
- held_values: bfloat16 [4096, 8, 8, 128], P('inst', None, 'tp')
- held_pages: int32 [4096], P('inst')
- decoded: bfloat16 [1, 8192], P(None, 'inst')
Inputs may be any that keep to these rules, and one draw needn't show every extreme that they name: `routes`: among the 32 pages of each instance no instance is named more than 1 times.
All inputs are finite; a program needn't handle non-finite values.
Results may differ from a plain program's by a relative error of at most 0.015.
Values may be sent and summed in bfloat16 or wider, within the bound.
A program may use at most 64 MiB of HBM per device.

v0:
```python
import functools
import math

import jax
import jax.numpy as jnp
from jax import lax
from jax.experimental import pallas as pl
from jax.experimental.pallas import tpu as pltpu
from jax.sharding import PartitionSpec as P

f32, bf16, i32 = jnp.float32, jnp.bfloat16, jnp.int32
MESH = pl.DeviceIdType.MESH
NEG = -1e30
NX, NY = 4, 8
HD, G = 128, 8
Q_DEV, CTX, PAGE, PG = 64, 256, 8, 32
R = Q_DEV * G
KROWS = CTX + Q_DEV + 16
VROWS = HD + 32
N = 2 * (CTX + Q_DEV)
SCALE = math.log2(math.e) / math.sqrt(HD)


def nt(a, b):
    return lax.dot_general(a, b, (((1,), (1,)), ((), ())), preferred_element_type=f32)


def nn(a, b):
    return lax.dot_general(a, b, (((1,), (0,)), ((), ())), preferred_element_type=f32)


def iota(shape, dim):
    return lax.broadcasted_iota(i32, shape, dim)


def unit(f):
    turn, group = (f - 1) % 3, (f - 1) // 3
    last = f >= 25
    block = jnp.where(turn == 0, 1, jnp.where(turn == 1, 2, 3))
    block = jnp.where(f == 3, 0, jnp.where(last, jnp.where(f == 25, 3, 0), block))
    k = jnp.where(turn == 2, group - 1, group)
    k = jnp.where(f == 3, 1, jnp.where(last, jnp.where(f == 25, 7, f - 24), k))
    own_first = f == 0
    return jnp.where(own_first, 0, block), jnp.where(own_first, 0, k)


def merge(parts):
    o, m, l = parts[:, 0:8], parts[:, 8:16], parts[:, 16:24]
    peak = jnp.max(m, axis=0)
    w = jnp.exp2(m - peak[None])
    return jnp.sum(w * o, axis=0), peak, jnp.sum(w * l, axis=0)


def kernel(
    nz,
    q_in, kc_in, vc_in, sk_in, sv_in, w_in, live_in, routes_in, dq_in, nk_in, nv_in,
    out, hk_out, hv_out, ids_out, dec_out,
    Kb, Vb, Db, Qb, vtmp, svb, wb, acc, m, l, Sa, Sb, Pa, Pb, al_a, al_b, mn_a, mn_b,
    Os, Or, Ts, Tr, PKs, PKr, Is, Ir, DX, Zb, ostage,
    lsem, sK, sV, sD, rK, rV, rD, sSV, rSV, sQ, rQ, sO, rO, sT, rT, sP, rP, sI, rI, sX, rX,
    sZ, rZ,
):
    me = lax.axis_index("inst")
    z = lax.axis_index("tp")
    c = me % 2
    x = (me // 2) % NX
    y = me // (2 * NX)

    def inst(yy, xx, cc):
        return (yy * NX + xx) * 2 + cc

    def ymod(v):
        return (v + 2 * NY) % NY

    sib = inst(y, x, 1 - c)
    up = inst(ymod(y + 1), x, c)
    down = inst(ymod(y - 1), x, c)
    xs = [x, (x + NX - 1) % NX, (x + 1) % NX, (x + 2) % NX]
    xpeer = [inst(y, v, c) for v in xs]
    mine = y * 2 + c

    def xblock(b):
        return (x + jnp.where(b == 1, NX - 1, jnp.where(b == 2, 1, jnp.where(b == 3, 2, 0)))) % NX

    def chip(k):
        return ymod(y + jnp.where(k == 7, 4, jnp.where(k % 2 == 1, -((k + 1) // 2), k // 2)))

    def remote(src, dst, ss, rs, to, zz=None):
        return pltpu.make_async_remote_copy(
            src_ref=src, dst_ref=dst, send_sem=ss, recv_sem=rs,
            device_id=(to, z if zz is None else zz), device_id_type=MESH,
        )

    loads = [
        pltpu.make_async_copy(kc_in, Kb.at[mine, 0:CTX], lsem.at[0]),
        pltpu.make_async_copy(sk_in, Kb.at[mine, CTX:CTX + Q_DEV], lsem.at[1]),
        pltpu.make_async_copy(sv_in, svb.at[c], lsem.at[2]),
        pltpu.make_async_copy(q_in, Qb.at[x], lsem.at[3]),
        pltpu.make_async_copy(vc_in, vtmp, lsem.at[4]),
        pltpu.make_async_copy(w_in, wb, lsem.at[5]),
    ]
    for load in loads:
        load.start()

    barrier = pltpu.get_barrier_semaphore()
    zpeers = [(z + j) % nz for j in range(1, nz)]
    for to in (sib, up, down, xpeer[1], xpeer[2], xpeer[3]):
        pl.semaphore_signal(barrier, inc=1, device_id=(to, z), device_id_type=MESH)
    for zz in zpeers:
        pl.semaphore_signal(barrier, inc=1, device_id=(me, zz), device_id_type=MESH)

    live_rows = live_in[0] * PAGE
    wide = iota((PG, CTX), 1) // PAGE == iota((PG, CTX), 0)
    per_token = jnp.sum(
        jnp.where(wide, routes_in[...].astype(f32), 0.0), axis=0, keepdims=True
    )
    row = iota((16, HD), 0)
    info = jnp.where(row == 0, live_rows.astype(f32), 0.0)
    info = jnp.where(row == 1, per_token[:, 0:HD], info)
    info = jnp.where(row == 2, per_token[:, HD:2 * HD], info)
    Kb[mine, CTX + Q_DEV:KROWS, :] = info.astype(bf16)
    for v in range(4):
        m[v] = jnp.full((8, R), NEG, f32)
        l[v] = jnp.zeros((8, R), f32)
        acc[v] = jnp.zeros((HD, R), f32)

    loads[0].wait()
    loads[1].wait()
    loads[2].wait()
    loads[3].wait()
    pl.semaphore_wait(barrier, 6 + nz - 1)

    def piece(kind, yy, way):
        buf, ss, rs = ((Kb, sK, rK), (Vb, sV, rV), (Db, sD, rD))[kind]
        s = yy * 2 + c
        return remote(buf.at[s], buf.at[s], ss.at[way, yy], rs.at[s], (up, down, sib)[way])

    def arrived(kind, s):
        buf, ss, rs = ((Kb, sK, rK), (Vb, sV, rV), (Db, sD, rD))[kind]
        remote(buf.at[s], buf.at[s], ss.at[0, 0], rs.at[s], sib).wait_recv()

    def qcopy(j):
        return remote(Qb.at[x], Qb.at[x], sQ.at[j], rQ.at[x], xpeer[j])

    span_copy = remote(svb.at[c], svb.at[c], sSV, rSV, sib)
    piece(0, y, 2).start()
    span_copy.start()
    piece(0, y, 0).start()
    piece(0, y, 1).start()
    qcopy(1).start()
    qcopy(2).start()

    loads[4].wait()
    Vb[mine, 0:HD, :] = vtmp[...].astype(f32).T.astype(bf16)
    remote(svb.at[1 - c], svb.at[1 - c], sSV, rSV, sib).wait_recv()
    both = jnp.concatenate([svb[0], svb[1]], axis=0).astype(f32).T
    half = jnp.where(c == 0, both[0:64], both[64:128])
    Vb[mine, HD:VROWS, :] = jnp.concatenate([half[0:32], half[32:64]], axis=1).astype(bf16)
    piece(1, y, 2).start()
    piece(1, y, 0).start()
    piece(1, y, 1).start()
    qcopy(3).start()

    dq = dq_in[...]
    s_cache = nt(dq, Kb[mine, 0:CTX, :]) * SCALE
    s_cache = jnp.where(iota((G, CTX), 1) < live_rows, s_cache, NEG)
    s_span = nt(dq, Kb[mine, CTX:CTX + Q_DEV, :]) * SCALE
    peak = jnp.maximum(
        jnp.max(s_cache, axis=1, keepdims=True), jnp.max(s_span, axis=1, keepdims=True)
    )
    p_cache, p_span = jnp.exp2(s_cache - peak), jnp.exp2(s_span - peak)
    weight = jnp.sum(p_cache, axis=1, keepdims=True) + jnp.sum(p_span, axis=1, keepdims=True)
    mixed = nt(p_cache.astype(bf16), Vb[mine, 0:HD, :]) + nn(p_span.astype(bf16), svb[c])
    Db[mine, 0:8, :] = mixed
    Db[mine, 8:16, :] = jnp.broadcast_to(peak, (8, HD))
    Db[mine, 16:24, :] = jnp.broadcast_to(weight, (8, HD))
    piece(2, y, 2).start()
    piece(2, y, 0).start()
    piece(2, y, 1).start()

    def scores(f, S, al, mn):
        block, k = unit(f)
        xq, yk = xblock(block), chip(k)
        q = Qb[xq]
        top = None
        for cc in range(2):
            s = yk * 2 + cc
            limit = Kb[s, CTX + Q_DEV:KROWS, :].astype(f32)[0:1, :]
            for h in range(2):
                sc = nt(Kb[s, h * HD:(h + 1) * HD, :], q)
                ok = (iota((HD, HD), 0) + h * HD).astype(f32) < limit
                sc = jnp.concatenate(
                    [jnp.where(ok, sc[:, t * HD:(t + 1) * HD], NEG) for t in range(R // HD)],
                    axis=1,
                )
                at = (cc * 2 + h) * HD
                S[at:at + HD, :] = sc
                best = jnp.max(sc.reshape(HD // 8, 8, R), axis=0)
                top = best if top is None else jnp.maximum(top, best)
                yield
        keys = jnp.concatenate(
            [Kb[yk * 2, CTX:CTX + Q_DEV, :], Kb[yk * 2 + 1, CTX:CTX + Q_DEV, :]], axis=0
        )
        sc = nt(keys, q)
        ahead = (inst(y, xq, c) - inst(yk, x, 0)) * Q_DEV
        sc = jnp.where(iota((HD, R), 0) <= iota((HD, R), 1) // G + ahead, sc, NEG)
        S[4 * HD:5 * HD, :] = sc
        top = jnp.maximum(top, jnp.max(sc.reshape(HD // 8, 8, R), axis=0))
        yield
        old = m[xq]
        new = jnp.maximum(old, jnp.max(top, axis=0, keepdims=True) * SCALE)
        al[...] = jnp.exp2(old - new)
        mn[...] = new
        m[xq] = new

    def weights(f, S, Pw, al, mn):
        block, _ = unit(f)
        xq = xblock(block)
        shrink, peak = al[...], mn[0:1, :]
        total = None
        for j in range(5):
            p = jnp.exp2(S[j * HD:(j + 1) * HD, :] * SCALE - peak)
            Pw[j * HD:(j + 1) * HD, :] = p.astype(bf16)
            part = jnp.sum(p.reshape(HD // 8, 8, R), axis=0)
            total = part if total is None else total + part
            yield
        l[xq] = l[xq] * shrink + total

    def values(f, Pw, al):
        block, k = unit(f)
        xq, yk = xblock(block), chip(k)
        shrink = al[0:1, :]
        s0, s1 = yk * 2, yk * 2 + 1
        span = jnp.concatenate(
            [Vb[s, HD:VROWS, t * HD:(t + 1) * HD] for s in (s0, s1) for t in range(2)], axis=0
        )
        vt = jnp.concatenate([Vb[s0, 0:HD, :], Vb[s1, 0:HD, :], span], axis=1)
        mix = nn(vt, Pw[...])
        for _ in range(4):
            yield
        acc[xq] = acc[xq] * shrink + mix

    def together(*stages):
        stages = list(stages)
        while stages:
            stages = [s for s in stages if next(s, stages) is None]

    def wait_chip(kind, k):
        arrived(kind, chip(k) * 2 + 1 - c)

    def pass_keys(d):
        yu, yd = ymod(y - d), ymod(y + d)
        arrived(0, yu * 2 + c)

        @pl.when(d < 4)
        def _():
            piece(0, yu, 0).start()

        piece(0, yu, 2).start()

        @pl.when(d < 4)
        def _():
            arrived(0, yd * 2 + c)

            @pl.when(d < 3)
            def _():
                piece(0, yd, 1).start()

            piece(0, yd, 2).start()

    def pass_values(d):
        yu, yd = ymod(y - d), ymod(y + d)
        for kind in (1, 2):
            @pl.when(d < 4)
            def _():
                arrived(kind, yu * 2 + c)

                @pl.when(d < 3)
                def _():
                    piece(kind, yu, 0).start()

                piece(kind, yu, 2).start()

            arrived(kind, yd * 2 + c)

            @pl.when(d < 4)
            def _():
                piece(kind, yd, 1).start()

            piece(kind, yd, 2).start()

    def pages(k):
        yk = chip(k)
        r, tok = iota((32, CTX), 0), iota((32, CTX), 1)
        to = (y * 2 * NX + (r // 8) * 2 + c).astype(f32)
        got_k, got_v = [], []
        for cc in range(2):
            s = yk * 2 + cc
            meta = Kb[s, CTX + Q_DEV:KROWS, :].astype(f32)
            limit = jnp.concatenate([meta[0:1, :]] * 2, axis=1)
            route = jnp.concatenate([meta[1:2, :], meta[2:3, :]], axis=1)
            hit = (route == to) & (tok % 8 == r % 8) & (tok.astype(f32) < limit)
            pick = jnp.where(hit, 1.0, 0.0)
            one = pick.astype(bf16)
            got_k.append(nn(one, Kb[s, 0:CTX, :]))
            got_v.append(nt(one, Vb[s, 0:HD, :]))
            number = inst(yk, x, cc) * PG + tok // PAGE + 1
            found = jnp.sum(jnp.where(hit, number, 0).astype(f32), axis=1, keepdims=True) - 1.0
            for v in range(NX):
                Is[v, pl.ds(s, 1), :] = jnp.broadcast_to(
                    found[v * 8:v * 8 + 1, :], (1, HD)
                ).astype(i32)
        for v in range(NX):
            for half, got in enumerate((got_k, got_v)):
                rows = jnp.concatenate([g[v * 8:v * 8 + 8, :] for g in got], axis=0)
                PKs[v, half, yk] = rows.astype(bf16)

    def send_pages():
        for j in (1, 2, 3):
            remote(PKs.at[xs[j]], PKr.at[x], sP.at[j], rP.at[x], xpeer[j]).start()
            remote(Is.at[xs[j]], Ir.at[x], sI.at[j], rI.at[x], xpeer[j]).start()

    def out_copies(j):
        return (
            remote(Os.at[xs[j]], Or.at[x], sO.at[j], rO.at[x], xpeer[j]),
            remote(Ts.at[xs[j]], Tr.at[x], sT.at[j], rT.at[x], xpeer[j]),
        )

    def send_out(j):
        v = xs[j]
        Os[v] = acc[v].astype(bf16)
        total = jnp.sum(l[v], axis=0, keepdims=True)
        Ts[v] = jnp.where(iota((8, R), 0) == 0, m[v], total)
        for copy in out_copies(j):
            copy.start()

    def decode_column():
        for k in range(8):
            arrived(2, chip(k) * 2 + 1 - c)
        o, peak, weight = merge(Db[...])
        DX[x, 0:8, :] = o
        DX[x, 8:16, :] = peak
        DX[x, 16:24, :] = weight
        for j in (1, 2, 3):
            remote(DX.at[x], DX.at[x], sX.at[j], rX.at[x], xpeer[j]).start()

    def decode_project():
        for j in (1, 2, 3):
            remote(DX.at[xs[j]], DX.at[xs[j]], sX.at[j], rX.at[xs[j]], xpeer[j]).wait_recv()
        o, peak, weight = merge(DX[...])
        own = jnp.sum(dq.astype(f32) * nk_in[...].astype(f32), axis=1, keepdims=True) * SCALE
        last = jnp.maximum(peak, own)
        shrink, extra = jnp.exp2(peak - last), jnp.exp2(own - last)
        weight = weight * shrink + extra
        o = o * shrink + extra.astype(bf16).astype(f32) * nv_in[...].astype(f32)
        attended = (o / weight).astype(bf16).astype(f32)
        head = iota((G, HD), 0)
        wide = jnp.concatenate(
            [jnp.where(head == h, attended, 0.0) for h in range(G)], axis=1
        ).astype(bf16)
        loads[5].wait()
        Zb[z] = nn(wide, wb[...])
        for j, zz in enumerate(zpeers):
            remote(Zb.at[z], Zb.at[z], sZ.at[j], rZ.at[z], me, zz).start()

    def hooks(f):
        @pl.when((f % 6 == 1) & (f < 20))
        def _():
            pass_keys((f + 5) // 6)

        @pl.when((f % 6 == 3) & (f < 22))
        def _():
            pass_values((f + 3) // 6)

        @pl.when(f == 1)
        def _():
            remote(Qb.at[xs[2]], Qb.at[xs[2]], sQ.at[2], rQ.at[xs[2]], xpeer[2]).wait_recv()

        @pl.when(f == 5)
        def _():
            remote(Qb.at[xs[3]], Qb.at[xs[3]], sQ.at[3], rQ.at[xs[3]], xpeer[3]).wait_recv()

        @pl.when((f == 2) | ((f % 3 == 0) & (f >= 6) & (f <= 21)))
        def _():
            wait_chip(0, jnp.where(f == 2, 1, f // 3))

        @pl.when((f == 4) | ((f % 3 == 2) & (f >= 8) & (f <= 23)))
        def _():
            wait_chip(1, jnp.where(f == 4, 1, (f - 2) // 3))

        @pl.when((f % 3 == 2) & (f <= 23))
        def _():
            pages((f - 2) // 3)

        @pl.when(f == 23)
        def _():
            send_pages()

        for j, at in ((1, 24), (2, 25), (3, 27)):
            @pl.when(f == at)
            def _():
                send_out(j)

        @pl.when(f == 24)
        def _():
            decode_column()

        @pl.when(f == 28)
        def _():
            decode_project()

    zero = jnp.int32(0)
    arrived(0, sib % 2 + y * 2)
    together(scores(zero, Sa, al_a, mn_a))
    remote(Qb.at[xs[1]], Qb.at[xs[1]], sQ.at[1], rQ.at[xs[1]], xpeer[1]).wait_recv()
    together(scores(zero + 1, Sb, al_b, mn_b), weights(zero, Sa, Pa, al_a, mn_a))
    arrived(1, sib % 2 + y * 2)

    def body(f, Sc, Sn, Pc, Pp, alc, alo, mnc, mno):
        hooks(f)
        together(
            values(f - 1, Pp, alo), weights(f, Sc, Pc, alc, mnc), scores(f + 1, Sn, alo, mno)
        )

    def pair(i, carry):
        f = 1 + 2 * i
        body(f, Sb, Sa, Pb, Pa, al_b, al_a, mn_b, mn_a)
        body(f + 1, Sa, Sb, Pa, Pb, al_a, al_b, mn_a, mn_b)
        return carry

    lax.fori_loop(0, 15, pair, 0)
    last = zero + 31
    together(values(last - 1, Pa, al_a), weights(last, Sb, Pb, al_b, mn_b))
    together(values(last, Pb, al_b))

    for j in (1, 2, 3):
        v = xs[j]
        remote(PKs.at[v], PKr.at[v], sP.at[j], rP.at[v], xpeer[j]).wait_recv()
        remote(Is.at[v], Ir.at[v], sI.at[j], rI.at[v], xpeer[j]).wait_recv()
    PKr[x] = PKs[x]
    Ir[x] = Is[x]
    stores = [
        pltpu.make_async_copy(PKr.at[v, half], ref.at[:, v], lsem.at[8 + half * NX + v])
        for half, ref in enumerate((hk_out, hv_out)) for v in range(NX)
    ]
    stores.append(pltpu.make_async_copy(Ir, ids_out, lsem.at[6]))
    for store in stores:
        store.start()

    for j, zz in enumerate(zpeers):
        remote(Zb.at[zz], Zb.at[zz], sZ.at[j], rZ.at[zz], me, zz).wait_recv()
    total = Zb[0]
    for v in range(1, nz):
        total = total + Zb[v]
    dec_out[...] = jnp.sum(total, axis=0, keepdims=True).astype(bf16)

    for j in (1, 2, 3):
        v = xs[j]
        remote(Os.at[v], Or.at[v], sO.at[j], rO.at[v], xpeer[j]).wait_recv()
        remote(Ts.at[v], Tr.at[v], sT.at[j], rT.at[v], xpeer[j]).wait_recv()
    peaks = [m[x][0:1, :]] + [Tr[xs[j], 0:1, :] for j in (1, 2, 3)]
    sums = [jnp.sum(l[x], axis=0, keepdims=True)] + [Tr[xs[j], 1:2, :] for j in (1, 2, 3)]
    peak = functools.reduce(jnp.maximum, peaks)
    shares = [jnp.exp2(p - peak) for p in peaks]
    whole = sum(w * s for w, s in zip(shares, sums))
    shares = [w / whole for w in shares]
    mix = acc[x] * shares[0]
    for j in (1, 2, 3):
        mix = mix + Or[xs[j]].astype(f32) * shares[j]
    ostage[...] = mix.T.astype(bf16)
    done = pltpu.make_async_copy(ostage, out, lsem.at[7])
    done.start()

    for kind in range(3):
        for d in range(4):
            if kind == 0 or d < 3:
                piece(kind, ymod(y - d), 0).wait_send()
            if d < 3 or kind > 0:
                piece(kind, ymod(y + d), 1).wait_send()
        for yy in range(NY):
            piece(kind, yy, 2).wait_send()
    span_copy.wait_send()
    for j in (1, 2, 3):
        qcopy(j).wait_send()
        for copy in out_copies(j):
            copy.wait_send()
        remote(PKs.at[xs[j]], PKr.at[x], sP.at[j], rP.at[x], xpeer[j]).wait_send()
        remote(Is.at[xs[j]], Ir.at[x], sI.at[j], rI.at[x], xpeer[j]).wait_send()
        remote(DX.at[x], DX.at[x], sX.at[j], rX.at[x], xpeer[j]).wait_send()
    for j, zz in enumerate(zpeers):
        remote(Zb.at[z], Zb.at[z], sZ.at[j], rZ.at[z], me, zz).wait_send()
    for store in stores:
        store.wait()
    done.wait()


def local(
    nz,
    query, key_cache, value_cache, span_keys, span_values, live_pages, routes,
    decode_query, new_key, new_value, w_out,
):
    hbm = pl.BlockSpec(memory_space=pl.ANY)
    vmem = pl.BlockSpec(memory_space=pltpu.VMEM)
    smem = pl.BlockSpec(memory_space=pltpu.SMEM)
    V, D = pltpu.VMEM, pltpu.SemaphoreType.DMA
    out, hk, hv, ids, decoded = pl.pallas_call(
        functools.partial(kernel, nz),
        out_shape=(
            jax.ShapeDtypeStruct((R, HD), bf16),
            jax.ShapeDtypeStruct((NY, NX, 16, HD), bf16),
            jax.ShapeDtypeStruct((NY, NX, 16, HD), bf16),
            jax.ShapeDtypeStruct((NX, 16, HD), i32),
            jax.ShapeDtypeStruct((1, HD), bf16),
        ),
        in_specs=[hbm] * 6 + [smem] + [vmem] * 4,
        out_specs=(hbm, hbm, hbm, hbm, vmem),
        scratch_shapes=[
            V((2 * NY, KROWS, HD), bf16), V((2 * NY, VROWS, CTX), bf16), V((2 * NY, 24, HD), f32),
            V((NX, R, HD), bf16), V((CTX, HD), bf16), V((2, Q_DEV, HD), bf16),
            V((HD * G, HD), bf16),
            V((NX, HD, R), f32), V((NX, 8, R), f32), V((NX, 8, R), f32),
            V((N, R), f32), V((N, R), f32), V((N, R), bf16), V((N, R), bf16),
            V((8, R), f32), V((8, R), f32), V((8, R), f32), V((8, R), f32),
            V((NX, HD, R), bf16), V((NX, HD, R), bf16), V((NX, 8, R), f32), V((NX, 8, R), f32),
            V((NX, 2, NY, 16, HD), bf16), V((NX, 2, NY, 16, HD), bf16),
            V((NX, 16, HD), i32), V((NX, 16, HD), i32),
            V((NX, 24, HD), f32), V((nz, 8, HD), f32), V((R, HD), bf16),
            D((16,)),
            D((3, NY)), D((3, NY)), D((3, NY)), D((2 * NY,)), D((2 * NY,)), D((2 * NY,)),
            D, D,
            D((NX,)), D((NX,)), D((NX,)), D((NX,)), D((NX,)), D((NX,)), D((NX,)), D((NX,)),
            D((NX,)), D((NX,)), D((NX,)), D((NX,)),
            D((nz,)), D((nz,)),
        ],
        compiler_params=pltpu.CompilerParams(
            collective_id=0, has_side_effects=True, vmem_limit_bytes=48 * 2**20
        ),
        cost_estimate=pl.CostEstimate(
            flops=4 * R * 64 * (CTX + Q_DEV) * HD, bytes_accessed=2**20,
            transcendentals=R * 64 * (CTX + Q_DEV),
        ),
        name="attend",
    )(
        query.reshape(R, HD), key_cache.reshape(CTX, HD), value_cache.reshape(CTX, HD),
        span_keys.reshape(Q_DEV, HD), span_values.reshape(Q_DEV, HD), w_out,
        live_pages, routes, decode_query, new_key, new_value,
    )
    held = ids[:, :, 0].reshape(NX, NY, 2).transpose(1, 0, 2).reshape(NX * NY * 2)
    return (
        out.reshape(Q_DEV, G, HD),
        hk.reshape(NX * NY * 2, PAGE, 1, HD),
        hv.reshape(NX * NY * 2, PAGE, 1, HD),
        held,
        decoded,
    )


def solution(mesh):
    return jax.shard_map(
        functools.partial(local, mesh.shape["tp"]),
        mesh=mesh,
        in_specs=(
            P("inst", "tp", None),
            P("inst", "tp", None),
            P("inst", "tp", None),
            P("inst", "tp", None),
            P("inst", "tp", None),
            P("inst"),
            P("inst", None),
            P("tp", None),
            P("tp", None),
            P("tp", None),
            P("tp", "inst"),
        ),
        out_specs=(
            P("inst", "tp", None),
            P("inst", None, "tp", None),
            P("inst", None, "tp", None),
            P("inst"),
            P(None, "inst"),
        ),
        check_vma=False,
    )
```

profile of v0, /device:TPU:6, one launch (start us, length us, event | category | flops | bytes accessed | tf_op | source)
XLA Modules:
  0.0 65.5 jit_solution(16197727701430606489)
XLA Ops:
  0.6 0.0 copy-start.4
  1.3 0.0 copy-start.6
  1.3 0.0 copy-start.7
  1.3 0.0 copy-start.8
  1.3 0.8 %copy.21.routes_in = s32[32,1]{1,0:T(8,128)S(1)} copy(s32[32,1]{0,1:T(1,128)} %param.17) | data formatting | bytes 256 | tf_op args[6]
  2.1 0.0 copy-done.4
  2.1 0.0 copy-done.6
  2.1 0.0 copy-done.7
  2.1 0.0 copy-done.8
  2.1 0.0 copy-start
  2.1 0.9 %copy-done = bf16[1024,128]{1,0:T(8,128)(2,1)S(1)} copy-done((bf16[1024,128]{1,0:T(8,128)(2,1)S(1)}, bf16[1024,128]{1,0:T(8,128)(2,1)}, u32[]{:S(2)}) %copy-start) | copy-done | bytes 262168
  3.1 0.0 copy-start.1
  3.1 0.9 %copy-done.1 = bf16[64,8,128]{2,1,0:T(8,128)(2,1)S(1)} copy-done((bf16[64,8,128]{2,1,0:T(8,128)(2,1)S(1)}, bf16[64,8,128]{2,1,0:T(8,128)(2,1)}, u32[]{:S(2)}) %copy-start.1) | copy-done | bytes 131096
  4.0 0.0 copy-start.2
  4.0 0.8 %copy-done.2 = bf16[256,1,128]{2,0,1:T(8,128)(2,1)S(1)} copy-done((bf16[256,1,128]{2,0,1:T(8,128)(2,1)S(1)}, bf16[256,1,128]{2,0,1:T(8,128)(2,1)}, u32[]{:S(2)}) %copy-start.2) | copy-done | bytes 65560
  4.8 0.0 copy-start.3
  4.8 0.8 %copy-done.3 = bf16[256,1,128]{2,0,1:T(8,128)(2,1)S(1)} copy-done((bf16[256,1,128]{2,0,1:T(8,128)(2,1)S(1)}, bf16[256,1,128]{2,0,1:T(8,128)(2,1)}, u32[]{:S(2)}) %copy-start.3) | copy-done | bytes 65560
  5.6 0.0 copy-start.5
  5.7 0.7 %copy-done.5 = bf16[64,1,128]{2,0,1:T(8,128)(2,1)S(1)} copy-done((bf16[64,1,128]{2,0,1:T(8,128)(2,1)S(1)}, bf16[64,1,128]{2,0,1:T(8,128)(2,1)}, u32[]{:S(2)}) %copy-start.5) | copy-done | bytes 16408
  6.4 55.7 %attend.1 = (bf16[512,128]{1,0:T(8,128)(2,1)S(1)}, bf16[8,4,16,128]{3,2,1,0:T(8,128)(2,1)S(1)}, bf16[8,4,16,128]{3,2,1,0:T(8,128)(2,1)S(1)}, s32[4,16,128]{2,1,0:T(8,128)S(1)}, bf16[1,128]{1,0:T(2,128)(2,1)S(1)}) custom-call(bf16[512,128]{1,0:T(8,128)(2,1)S(1)} %bitcast.20, bf16[256,128]{1,0:T(8,128)(2,1)S(1)} %bitcast.21, bf16[256,128]{1,0:T(8,128)(2,1)S(1)} %bitcast.22, ...), custom_call_target="tpu_custom_call" | custom-call | flops 5368709120 | bytes 1048576 | tf_op jit(solution)/shard_map/attend/pallas_call | solution.py:506
  62.1 0.2 copy.22
  62.3 0.1 copy.23
  62.4 0.6 reshape.45
  63.1 0.7 copy.31
  63.7 0.7 copy.32
  64.4 0.7 copy.33
  65.0 0.5 copy.34
Async XLA Ops:
  0.6 1.5 %copy-start.4 = (bf16[64,1,128]{2,0,1:T(8,128)(2,1)S(1)}, bf16[64,1,128]{2,0,1:T(8,128)(2,1)}, u32[]{:S(2)}) copy-start(bf16[64,1,128]{2,0,1:T(8,128)(2,1)} %param.14) | copy-start | bytes 49156
  1.3 0.8 %copy-start.6 = (bf16[8,128]{1,0:T(8,128)(2,1)S(1)}, bf16[8,128]{1,0:T(8,128)(2,1)}, u32[]{:S(2)}) copy-start(bf16[8,128]{1,0:T(8,128)(2,1)} %dq_in.1) | copy-start | bytes 6148
  1.3 0.8 %copy-start.7 = (bf16[1,128]{1,0:T(2,128)(2,1)S(1)}, bf16[1,128]{1,0:T(2,128)(2,1)}, u32[]{:S(2)}) copy-start(bf16[1,128]{1,0:T(2,128)(2,1)} %nk_in.1) | copy-start | bytes 772
  1.3 0.8 %copy-start.8 = (bf16[1,128]{1,0:T(2,128)(2,1)S(1)}, bf16[1,128]{1,0:T(2,128)(2,1)}, u32[]{:S(2)}) copy-start(bf16[1,128]{1,0:T(2,128)(2,1)} %nv_in.1) | copy-start | bytes 772
  2.1 1.0 %copy-start = (bf16[1024,128]{1,0:T(8,128)(2,1)S(1)}, bf16[1024,128]{1,0:T(8,128)(2,1)}, u32[]{:S(2)}) copy-start(bf16[1024,128]{1,0:T(8,128)(2,1)} %w_in.1) | copy-start | bytes 786436
  3.1 0.9 %copy-start.1 = (bf16[64,8,128]{2,1,0:T(8,128)(2,1)S(1)}, bf16[64,8,128]{2,1,0:T(8,128)(2,1)}, u32[]{:S(2)}) copy-start(bf16[64,8,128]{2,1,0:T(8,128)(2,1)} %param.11) | copy-start | bytes 393220
  4.0 0.8 %copy-start.2 = (bf16[256,1,128]{2,0,1:T(8,128)(2,1)S(1)}, bf16[256,1,128]{2,0,1:T(8,128)(2,1)}, u32[]{:S(2)}) copy-start(bf16[256,1,128]{2,0,1:T(8,128)(2,1)} %param.12) | copy-start | bytes 196612
  4.8 0.8 %copy-start.3 = (bf16[256,1,128]{2,0,1:T(8,128)(2,1)S(1)}, bf16[256,1,128]{2,0,1:T(8,128)(2,1)}, u32[]{:S(2)}) copy-start(bf16[256,1,128]{2,0,1:T(8,128)(2,1)} %param.13) | copy-start | bytes 196612
  5.6 0.7 %copy-start.5 = (bf16[64,1,128]{2,0,1:T(8,128)(2,1)S(1)}, bf16[64,1,128]{2,0,1:T(8,128)(2,1)}, u32[]{:S(2)}) copy-start(bf16[64,1,128]{2,0,1:T(8,128)(2,1)} %param.15) | copy-start | bytes 49156
where the time goes:
time: 65.9 us; the launch traced here: 65.5 us
  Pallas kernels  55.7 us (85%)
  local copies, waits for them, and re-layouts  8.45 us (13%)
  between operations  1.36 us (2%)
    pallas_call x1, Pallas kernels, local(): pl.pallas_call(functools.partial(kernel, nz), out_shape=(jax.ShapeDtypeSt...  55.7 us
    unnamed x23, local copies, waits for them, and re-layouts  7.49 us

commit v1 on v0

v1 whole, which is shorter than its diff:
```python
import functools
import math

import jax
import jax.numpy as jnp
from jax import lax
from jax.experimental import pallas as pl
from jax.experimental.pallas import tpu as pltpu
from jax.sharding import PartitionSpec as P

f32, bf16, i32 = jnp.float32, jnp.bfloat16, jnp.int32
MESH = pl.DeviceIdType.MESH
NEG = -1e30
LIMIT = 60 * 2**20
NX, NY = 4, 8
HD, G = 128, 8
Q_DEV, CTX, PAGE, PG = 64, 256, 8, 32
R = Q_DEV * G
KROWS = CTX + Q_DEV + 16
VROWS = HD + 32
N = 6 * (CTX + Q_DEV)
SCALE = math.log2(math.e) / math.sqrt(HD)


def nt(a, b):
    return lax.dot_general(a, b, (((1,), (1,)), ((), ())), preferred_element_type=f32)


def nn(a, b):
    return lax.dot_general(a, b, (((1,), (0,)), ((), ())), preferred_element_type=f32)


def iota(shape, dim):
    return lax.broadcasted_iota(i32, shape, dim)


NEAR, MID, FAR, LAST = (0, 1, 2), (3, 4), (5, 6), (7,)
UNITS = (
    (1, NEAR), (2, NEAR), (0, NEAR), (1, MID), (2, MID), (3, NEAR), (3, MID), (1, FAR), (2, FAR),
    (3, FAR), (3, LAST), (1, LAST), (2, LAST), (0, MID), (0, FAR + LAST),
)


def merge(parts):
    o, m, l = parts[:, 0:8], parts[:, 8:16, 0:1], parts[:, 8:16, HD // 2:HD // 2 + 1]
    peak = jnp.max(m, axis=0)
    w = jnp.exp2(m - peak[None])
    return jnp.sum(w * o, axis=0), peak, jnp.sum(w * l, axis=0)


def kernel(
    nz,
    q_in, kc_in, vc_in, sk_in, sv_in, w_in, live_hbm, routes_hbm, dq_hbm, nk_hbm, nv_hbm,
    out, hk_out, hv_out, ids_out, dec_out,
    live_in, routes_in, dq_in, nk_in, nv_in, held_stage, dec_stage, Kb, Vb, Db, Qb, vtmp, svb, wb, acc, m, l, Sa, Sb, Pa, Pb, al_a, al_b, mn_a, mn_b,
    Os, Or, Ts, Tr, PKs, PKr, Is, Ir, DX, Zb, ostage,
    lsem, sR, rR, sSV, rSV, sQ, rQ, sO, rO, sT, rT, sP, rP, sI, rI, sX, rX,
    sZ, rZ,
):
    me = lax.axis_index("inst")
    z = lax.axis_index("tp")
    c = me % 2
    x = (me // 2) % NX
    y = me // (2 * NX)

    def inst(yy, xx, cc):
        return (yy * NX + xx) * 2 + cc

    def ymod(v):
        return (v + 2 * NY) % NY

    sib = inst(y, x, 1 - c)
    up = inst(ymod(y + 1), x, c)
    down = inst(ymod(y - 1), x, c)
    xs = [x, (x + NX - 1) % NX, (x + 1) % NX, (x + 2) % NX]
    xpeer = [inst(y, v, c) for v in xs]
    mine = y * 2 + c

    around = [ymod(y + v) for v in range(NY)]

    def chip(k):
        return around[(4 if k == 7 else -((k + 1) // 2) if k % 2 else k // 2) % NY]

    def remote(src, dst, ss, rs, to, zz=None):
        return pltpu.make_async_remote_copy(
            src_ref=src, dst_ref=dst, send_sem=ss, recv_sem=rs,
            device_id=(to, z if zz is None else zz), device_id_type=MESH,
        )

    loads = [
        pltpu.make_async_copy(kc_in, Kb.at[mine, 0:CTX], lsem.at[0]),
        pltpu.make_async_copy(sk_in, Kb.at[mine, CTX:CTX + Q_DEV], lsem.at[1]),
        pltpu.make_async_copy(sv_in, svb.at[c], lsem.at[2]),
        pltpu.make_async_copy(q_in, Qb.at[x], lsem.at[3]),
        pltpu.make_async_copy(vc_in, vtmp, lsem.at[4]),
        pltpu.make_async_copy(w_in, wb, lsem.at[5]),
        pltpu.make_async_copy(live_hbm, live_in, lsem.at[16]),
        pltpu.make_async_copy(routes_hbm, routes_in, lsem.at[17]),
        pltpu.make_async_copy(dq_hbm, dq_in, lsem.at[18]),
        pltpu.make_async_copy(nk_hbm, nk_in, lsem.at[19]),
        pltpu.make_async_copy(nv_hbm, nv_in, lsem.at[20]),
    ]
    for load in loads:
        load.start()

    barrier = pltpu.get_barrier_semaphore()
    zpeers = [(z + j) % nz for j in range(1, nz)]
    for to in (sib, up, down, xpeer[1], xpeer[2], xpeer[3]):
        pl.semaphore_signal(barrier, inc=1, device_id=(to, z), device_id_type=MESH)
    for zz in zpeers:
        pl.semaphore_signal(barrier, inc=1, device_id=(me, zz), device_id_type=MESH)

    loads[6].wait()
    loads[7].wait()
    live_rows = live_in[0:1, 0:1] * PAGE
    wide = iota((PG, CTX), 1) // PAGE == iota((PG, CTX), 0)
    per_token = nn(
        jnp.broadcast_to(routes_in[...].astype(f32), (8, PG)).astype(bf16),
        jnp.where(wide, 1.0, 0.0).astype(bf16),
    )[0:1, :]
    row = iota((16, HD), 0)
    info = jnp.where(row == 0, live_rows.astype(f32), 0.0)
    info = jnp.where(row == 1, per_token[:, 0:HD], info)
    info = jnp.where(row == 2, per_token[:, HD:2 * HD], info)
    Kb[mine, CTX + Q_DEV:KROWS, :] = info.astype(bf16)
    for v in range(4):
        Is[v] = jnp.full((8, HD), -1, i32)
        m[v] = jnp.full((8, R), NEG, f32)
        l[v] = jnp.zeros((8, R), f32)
        acc[v] = jnp.zeros((HD, R), f32)

    loads[0].wait()
    loads[1].wait()
    loads[2].wait()
    loads[3].wait()
    pl.semaphore_wait(barrier, 6 + nz - 1)

    def part(p, s):
        if p < 2:
            return Kb.at[s, 176:KROWS] if p else Kb.at[s, 0:176]
        if p < 4:
            return Vb.at[s, VROWS // 2:VROWS] if p == 3 else Vb.at[s, 0:VROWS // 2]
        return Db.at[s]

    def piece(p, yy, way):
        s = yy * 2 + c
        return remote(part(p, s), part(p, s), sR.at[p, way, yy], rR.at[p, s], (up, down, sib)[way])

    def arrived(p, s):
        remote(part(p, s), part(p, s), sR.at[p, 0, 0], rR.at[p, s], sib).wait_recv()

    def qcopy(j):
        return remote(Qb.at[x], Qb.at[x], sQ.at[j], rQ.at[x], xpeer[j])

    span_copy = remote(svb.at[c], svb.at[c], sSV, rSV, sib)
    def send_own(p):
        for way in (0, 1, 2):
            piece(p, y, way).start()

    span_copy.start()
    send_own(0)
    send_own(1)
    qcopy(1).start()
    qcopy(2).start()
    loads[4].wait()
    Vb[mine, 0:HD, :] = vtmp[...].astype(f32).T.astype(bf16)
    remote(svb.at[1 - c], svb.at[1 - c], sSV, rSV, sib).wait_recv()
    both = jnp.concatenate([svb[0], svb[1]], axis=0).astype(f32).T
    half = jnp.where(c == 0, both[0:64], both[64:128])
    Vb[mine, HD:VROWS, :] = jnp.concatenate([half[0:32], half[32:64]], axis=1).astype(bf16)

    def sent(p):
        for way in (0, 1):
            piece(p, y, way).wait_send()

    sent(0)
    send_own(2)
    sent(1)
    send_own(3)

    loads[8].wait()
    dq = dq_in[...]
    s_cache = nt(dq, Kb[mine, 0:CTX, :]) * SCALE
    s_cache = jnp.where(iota((G, CTX), 1) < live_rows, s_cache, NEG)
    s_span = nt(dq, Kb[mine, CTX:CTX + Q_DEV, :]) * SCALE
    peak = jnp.maximum(
        jnp.max(s_cache, axis=1, keepdims=True), jnp.max(s_span, axis=1, keepdims=True)
    )
    p_cache, p_span = jnp.exp2(s_cache - peak), jnp.exp2(s_span - peak)
    weight = jnp.sum(p_cache, axis=1, keepdims=True) + jnp.sum(p_span, axis=1, keepdims=True)
    mixed = nt(p_cache.astype(bf16), Vb[mine, 0:HD, :]) + nn(p_span.astype(bf16), svb[c])
    Db[mine, 0:8, :] = mixed
    Db[mine, 8:16, :] = jnp.where(iota((8, HD), 1) < HD // 2, peak, weight)

    send_own(4)
    qcopy(1).wait_send()
    qcopy(2).wait_send()
    qcopy(3).start()

    bufs = ((Sa, Pa, al_a, mn_a), (Sb, Pb, al_b, mn_b))

    def scores(f):
        block, chips = UNITS[f]
        S, _, al, mn = bufs[f % 2]
        xq, chips = xs[block], [chip(k) for k in chips]
        q = Qb[xq]
        top, at = None, 0
        for yk in chips:
            for cc in range(2):
                s = yk * 2 + cc
                limit = Kb[s, CTX + Q_DEV:KROWS, :].astype(f32)[0:1, :]
                sc = nt(Kb[s, 0:CTX, :], q)
                ok = iota((CTX, HD), 0).astype(f32) < limit
                sc = jnp.concatenate(
                    [jnp.where(ok, sc[:, t * HD:(t + 1) * HD], NEG) for t in range(R // HD)],
                    axis=1,
                )
                S[at:at + CTX, :] = sc
                at += CTX
                best = jnp.max(sc.reshape(CTX // 8, 8, R), axis=0)
                top = best if top is None else jnp.maximum(top, best)
                yield
        for yk in chips:
            keys = jnp.concatenate(
                [Kb[yk * 2, CTX:CTX + Q_DEV, :], Kb[yk * 2 + 1, CTX:CTX + Q_DEV, :]], axis=0
            )
            sc = nt(keys, q)
            ahead = (inst(y, xq, c) - inst(yk, x, 0)) * Q_DEV
            sc = jnp.where(iota((HD, R), 0) <= iota((HD, R), 1) // G + ahead, sc, NEG)
            S[at:at + HD, :] = sc
            at += HD
            top = jnp.maximum(top, jnp.max(sc.reshape(HD // 8, 8, R), axis=0))
        yield
        old = m[xq]
        new = jnp.maximum(old, jnp.max(top, axis=0, keepdims=True) * SCALE)
        al[...] = jnp.exp2(old - new)
        mn[...] = new
        m[xq] = new

    def weights(f):
        block, chips = UNITS[f]
        S, Pw, al, mn = bufs[f % 2]
        xq = xs[block]
        shrink, peak = al[...], mn[0:1, :]
        total = None
        rows = len(chips) * 2 * (CTX + Q_DEV)
        for at in range(0, rows, CTX):
            n = min(CTX, rows - at)
            p = jnp.exp2(S[at:at + n, :] * SCALE - peak)
            Pw[at:at + n, :] = p.astype(bf16)
            part = jnp.sum(p.reshape(n // 8, 8, R), axis=0)
            total = part if total is None else total + part
            yield
        l[xq] = l[xq] * shrink + total

    def values(f):
        block, chips = UNITS[f]
        _, Pw, al, _ = bufs[f % 2]
        xq, chips = xs[block], [chip(k) for k in chips]
        shrink = al[0:1, :]
        cached = [Vb[yk * 2 + cc, 0:HD, :] for yk in chips for cc in range(2)]
        spans = [
            jnp.concatenate(
                [
                    Vb[yk * 2 + cc, HD:VROWS, t * HD:(t + 1) * HD]
                    for cc in range(2) for t in range(2)
                ],
                axis=0,
            )
            for yk in chips
        ]
        mix = nn(
            jnp.concatenate(cached + spans, axis=1), Pw[0:len(chips) * 2 * (CTX + Q_DEV), :]
        )
        for _ in range(4):
            yield
        acc[xq] = acc[xq] * shrink + mix

    def together(*stages):
        stages = list(stages)
        while stages:
            stages = [s for s in stages if next(s, stages) is None]

    def wait_chip(pieces, k):
        for p in pieces:
            arrived(p, chip(k) * 2 + 1 - c)

    def pass_keys(p, d):
        yu, yd = around[-d], around[d]
        arrived(p, yu * 2 + c)
        piece(p, yu, 2).start()

        if d < 4:
            piece(p, yu, 0).start()
            arrived(p, yd * 2 + c)
            piece(p, yd, 2).start()

            if d < 3:
                piece(p, yd, 1).start()

    def pass_values(p, d):
        yu, yd = around[-d], around[d]
        arrived(p, yd * 2 + c)
        piece(p, yd, 2).start()

        if d < 4:
            piece(p, yd, 1).start()
            arrived(p, yu * 2 + c)
            piece(p, yu, 2).start()

            if d < 3:
                piece(p, yu, 0).start()

    def page_copy(j, yk):
        return remote(
            PKs.at[xs[j], yk], PKr.at[x, yk], sP.at[j, yk], rP.at[x, yk], xpeer[j]
        )

    def pages(k):
        yk = chip(k)
        r, tok = iota((32, CTX), 0), iota((32, CTX), 1)
        to = (y * 2 * NX + (r // 8) * 2 + c).astype(f32)
        got_k, got_v = [], []
        for cc in range(2):
            s = yk * 2 + cc
            meta = Kb[s, CTX + Q_DEV:KROWS, :].astype(f32)
            limit = jnp.concatenate([meta[0:1, :]] * 2, axis=1)
            route = jnp.concatenate([meta[1:2, :], meta[2:3, :]], axis=1)
            hit = (route == to) & (tok % 8 == r % 8) & (tok.astype(f32) < limit)
            one = jnp.where(hit, 1.0, 0.0).astype(bf16)
            got_k.append(nn(one, Kb[s, 0:CTX, :]))
            got_v.append(nt(one, Vb[s, 0:HD, :]))
            number = (inst(yk, x, cc) * PG + tok // PAGE + 1).astype(f32)
            found = jnp.sum(jnp.where(hit, number, 0.0), axis=1, keepdims=True) - 1.0
            here = iota((8, HD), 1) == inst(yk, x, cc)
            for v in range(NX):
                Is[v] = jnp.where(here, found[v * 8:v * 8 + 8, :].astype(i32), Is[v])
        for v in range(NX):
            for half, got in enumerate((got_k, got_v)):
                rows = jnp.concatenate([g[v * 8:v * 8 + 8, :] for g in got], axis=0)
                PKs[v, yk, half] = rows.astype(bf16)
        for j in (1, 2, 3):
            page_copy(j, yk).start()

    def send_ids():
        for j in (1, 2, 3):
            remote(Is.at[xs[j]], Ir.at[x], sI.at[j], rI.at[x], xpeer[j]).start()

    def out_copies(j):
        return (
            remote(Os.at[xs[j]], Or.at[x], sO.at[j], rO.at[x], xpeer[j]),
            remote(Ts.at[xs[j]], Tr.at[x], sT.at[j], rT.at[x], xpeer[j]),
        )

    def send_out(j):
        v = xs[j]
        Os[v] = acc[v].astype(bf16)
        top, total = m[v][0:1, :], jnp.sum(l[v], axis=0, keepdims=True)
        Ts[v] = jnp.concatenate(
            [row[:, t * HD:(t + 1) * HD] for row in (top, total) for t in range(R // HD)], axis=0
        )
        for copy in out_copies(j):
            copy.start()

    def decode_column():
        for k in range(8):
            arrived(4, chip(k) * 2 + 1 - c)
        o, peak, weight = merge(Db[...])
        DX[x, 0:8, :] = o
        DX[x, 8:16, :] = jnp.where(iota((8, HD), 1) < HD // 2, peak, weight)
        for j in (1, 2, 3):
            remote(DX.at[x], DX.at[x], sX.at[j], rX.at[x], xpeer[j]).start()

    def decode_project():
        for n in (5, 9, 10):
            loads[n].wait()
        for j in (1, 2, 3):
            remote(DX.at[xs[j]], DX.at[xs[j]], sX.at[j], rX.at[xs[j]], xpeer[j]).wait_recv()
        o, peak, weight = merge(DX[...])
        own = jnp.sum(dq.astype(f32) * nk_in[...].astype(f32), axis=1, keepdims=True) * SCALE
        last = jnp.maximum(peak, own)
        shrink, extra = jnp.exp2(peak - last), jnp.exp2(own - last)
        weight = weight * shrink + extra
        o = o * shrink + extra.astype(bf16).astype(f32) * nv_in[...].astype(f32)
        attended = (o / weight).astype(bf16).astype(f32)
        head = iota((G, HD), 0)
        wide = jnp.concatenate(
            [jnp.where(head == h, attended, 0.0) for h in range(G)], axis=1
        ).astype(bf16)
        Zb[z] = nn(wide, wb[...])
        for j, zz in enumerate(zpeers):
            remote(Zb.at[z], Zb.at[z], sZ.at[j], rZ.at[z], me, zz).start()

    def arrived_query(j):
        remote(Qb.at[xs[j]], Qb.at[xs[j]], sQ.at[j], rQ.at[xs[j]], xpeer[j]).wait_recv()

    def before(f):
        if f == 0:
            pass_values(2, 1)
            pass_values(3, 1)
        if f == 1:
            for k in (0, 1, 2):
                wait_chip((2, 3), k)
        if f in (2, 4, 7):
            pass_keys(0, f // 2 + 1 if f < 7 else 4)
            pass_keys(1, f // 2 + 1 if f < 7 else 4)
        if f == 2:
            for k in (0, 1, 2):
                pages(k)
            for k in (3, 4):
                wait_chip((0, 1), k)
        if f in (3, 6, 9):
            pass_values(2, f // 3 + 1)
            pass_values(3, f // 3 + 1)
        if f in (2, 5, 8, 10):
            pass_values(4, {2: 1, 5: 2, 8: 3, 10: 4}[f])
        if f == 4:
            arrived_query(3)
            for k in (3, 4):
                wait_chip((2, 3), k)
        if f == 5:
            pages(3)
            pages(4)
        if f == 6:
            for k in (5, 6):
                wait_chip((0, 1), k)
        if f == 8:
            for k in (5, 6):
                wait_chip((2, 3), k)
        if f == 9:
            wait_chip((0, 1), 7)
        if f == 10:
            pages(5)
            pages(6)
        if f == 11:
            wait_chip((2, 3), 7)
            decode_column()
        if f == 12:
            send_out(3)
            pages(7)
            send_ids()
        if f == 13:
            send_out(1)
        if f == 14:
            send_out(2)
            decode_project()

    pass_keys(0, 1)
    pass_keys(1, 1)
    arrived_query(1)
    for k in (0, 1, 2):
        wait_chip((0, 1), k)
    together(scores(0))
    arrived_query(2)
    end = len(UNITS)
    for f in range(end):
        before(f)
        stages = [values(f - 1)] if f else []
        stages.append(weights(f))
        if f + 1 < end:
            stages.append(scores(f + 1))
        together(*stages)
    together(values(end - 1))

    for j in (1, 2, 3):
        v = xs[j]
        for yk in range(NY):
            remote(
                PKs.at[v, yk], PKr.at[v, yk], sP.at[j, yk], rP.at[v, yk], xpeer[j]
            ).wait_recv()
        remote(Is.at[v], Ir.at[v], sI.at[j], rI.at[v], xpeer[j]).wait_recv()
    PKr[x] = PKs[x]
    Ir[x] = Is[x]
    stores = [
        pltpu.make_async_copy(PKr.at[v, :, half], ref.at[:, v], lsem.at[8 + half * NX + v])
        for half, ref in enumerate((hk_out, hv_out)) for v in range(NX)
    ]
    for store in stores:
        store.start()
    held = functools.reduce(jnp.maximum, [Ir[v] for v in range(NX)])
    held_stage[...] = held[0:1, 0:NX * NY * 2]
    stores.append(pltpu.make_async_copy(held_stage, ids_out, lsem.at[21]))
    stores[-1].start()

    for j, zz in enumerate(zpeers):
        remote(Zb.at[zz], Zb.at[zz], sZ.at[j], rZ.at[zz], me, zz).wait_recv()
    total = Zb[0]
    for v in range(1, nz):
        total = total + Zb[v]
    dec_stage[...] = jnp.sum(total, axis=0, keepdims=True).astype(bf16)
    stores.append(pltpu.make_async_copy(dec_stage, dec_out, lsem.at[22]))
    stores[-1].start()

    for j in (1, 2, 3):
        v = xs[j]
        remote(Os.at[v], Or.at[v], sO.at[j], rO.at[v], xpeer[j]).wait_recv()
        remote(Ts.at[v], Tr.at[v], sT.at[j], rT.at[v], xpeer[j]).wait_recv()
    def stat(j, first):
        return jnp.concatenate(
            [Tr[xs[j], first + t:first + t + 1, :] for t in range(R // HD)], axis=1
        )

    peaks = [m[x][0:1, :]] + [stat(j, 0) for j in (1, 2, 3)]
    sums = [jnp.sum(l[x], axis=0, keepdims=True)] + [stat(j, 4) for j in (1, 2, 3)]
    peak = functools.reduce(jnp.maximum, peaks)
    shares = [jnp.exp2(p - peak) for p in peaks]
    whole = sum(w * s for w, s in zip(shares, sums))
    shares = [w / whole for w in shares]
    mix = acc[x] * shares[0]
    for j in (1, 2, 3):
        mix = mix + Or[xs[j]].astype(f32) * shares[j]
    ostage[...] = mix.T.astype(bf16)
    done = pltpu.make_async_copy(ostage, out, lsem.at[7])
    done.start()

    for p in range(5):
        for d in range(4):
            if d == 0 and p < 2:
                continue
            if p < 2 or d < 3:
                piece(p, around[-d], 0).wait_send()
            if p > 1 or d < 3:
                piece(p, around[d], 1).wait_send()
        for yy in range(NY):
            piece(p, yy, 2).wait_send()
    span_copy.wait_send()
    for j in (1, 2, 3):
        if j == 3:
            qcopy(j).wait_send()
        for copy in out_copies(j):
            copy.wait_send()
        for yk in range(NY):
            page_copy(j, yk).wait_send()
        remote(Is.at[xs[j]], Ir.at[x], sI.at[j], rI.at[x], xpeer[j]).wait_send()
        remote(DX.at[x], DX.at[x], sX.at[j], rX.at[x], xpeer[j]).wait_send()
    for j, zz in enumerate(zpeers):
        remote(Zb.at[z], Zb.at[z], sZ.at[j], rZ.at[z], me, zz).wait_send()
    for store in stores:
        store.wait()
    done.wait()


def write(*refs):
    ins, outs, stages, sem = refs[:5], refs[5:10], refs[10:15], refs[15]
    first = [pltpu.make_async_copy(a, b, sem.at[0, n]) for n, (a, b) in enumerate(zip(ins, stages))]
    second = [pltpu.make_async_copy(a, b, sem.at[1, n]) for n, (a, b) in enumerate(zip(stages, outs))]
    for copy in first:
        copy.start()
    for copy, then in zip(first, second):
        copy.wait()
        then.start()
    for copy in second:
        copy.wait()


def local(
    nz,
    query, key_cache, value_cache, span_keys, span_values, live_pages, routes,
    decode_query, new_key, new_value, w_out,
):
    hbm = pl.BlockSpec(memory_space=pltpu.HBM)
    whole = pl.BlockSpec(memory_space=pl.ANY)
    V, D = pltpu.VMEM, pltpu.SemaphoreType.DMA
    out, hk, hv, ids, decoded = pl.pallas_call(
        functools.partial(kernel, nz),
        out_shape=(
            jax.ShapeDtypeStruct((R, HD), bf16),
            jax.ShapeDtypeStruct((NY, NX, 16, HD), bf16),
            jax.ShapeDtypeStruct((NY, NX, 16, HD), bf16),
            jax.ShapeDtypeStruct((1, NX * NY * 2), i32),
            jax.ShapeDtypeStruct((1, HD), bf16),
        ),
        in_specs=[hbm] * 11,
        out_specs=[whole] * 5,
        scratch_shapes=[
            V((1, 1), i32), V((1, PG), i32), V((G, HD), bf16), V((1, HD), bf16), V((1, HD), bf16),
            V((1, NX * NY * 2), i32), V((1, HD), bf16),
            V((2 * NY, KROWS, HD), bf16), V((2 * NY, VROWS, CTX), bf16), V((2 * NY, 16, HD), f32),
            V((NX, R, HD), bf16), V((CTX, HD), bf16), V((2, Q_DEV, HD), bf16),
            V((HD * G, HD), bf16),
            V((NX, HD, R), f32), V((NX, 8, R), f32), V((NX, 8, R), f32),
            V((N, R), f32), V((N, R), f32), V((N, R), bf16), V((N, R), bf16),
            V((8, R), f32), V((8, R), f32), V((8, R), f32), V((8, R), f32),
            V((NX, HD, R), bf16), V((NX, HD, R), bf16), V((NX, 8, HD), f32), V((NX, 8, HD), f32),
            V((NX, NY, 2, 16, HD), bf16), V((NX, NY, 2, 16, HD), bf16),
            V((NX, 8, HD), i32), V((NX, 8, HD), i32),
            V((NX, 16, HD), f32), V((nz, 8, HD), f32), V((R, HD), bf16),
            D((23,)),
            D((5, 3, NY)), D((5, 2 * NY)),
            D, D,
            D((NX,)), D((NX,)), D((NX,)), D((NX,)), D((NX,)), D((NX,)), D((NX, NY)), D((NX, NY)),
            D((NX,)), D((NX,)), D((NX,)), D((NX,)),
            D((nz,)), D((nz,)),
        ],
        compiler_params=pltpu.CompilerParams(
            collective_id=0, has_side_effects=True, vmem_limit_bytes=LIMIT
        ),
        cost_estimate=pl.CostEstimate(
            flops=4 * R * 64 * (CTX + Q_DEV) * HD, bytes_accessed=2**20,
            transcendentals=R * 64 * (CTX + Q_DEV),
        ),
        name="attend",
    )(
        query.reshape(R, HD), key_cache.reshape(CTX, HD), value_cache.reshape(CTX, HD),
        span_keys.reshape(Q_DEV, HD), span_values.reshape(Q_DEV, HD), w_out,
        live_pages.reshape(1, 1), routes.reshape(1, PG), decode_query, new_key, new_value,
    )
    results = (out, hk, hv, ids, decoded)
    out, hk, hv, ids, decoded = pl.pallas_call(
        write,
        out_shape=tuple(jax.ShapeDtypeStruct(a.shape, a.dtype) for a in results),
        in_specs=[whole] * 5,
        out_specs=[whole] * 5,
        scratch_shapes=[V(a.shape, a.dtype) for a in results] + [D((2, 5))],
        compiler_params=pltpu.CompilerParams(vmem_limit_bytes=LIMIT),
        name="write",
    )(*results)
    return (
        out.reshape(Q_DEV, G, HD),
        hk.reshape(NX * NY * 2, PAGE, 1, HD),
        hv.reshape(NX * NY * 2, PAGE, 1, HD),
        ids.reshape(NX * NY * 2),
        decoded,
    )


def solution(mesh):
    return jax.shard_map(
        functools.partial(local, mesh.shape["tp"]),
        mesh=mesh,
        in_specs=(
            P("inst", "tp", None),
            P("inst", "tp", None),
            P("inst", "tp", None),
            P("inst", "tp", None),
            P("inst", "tp", None),
            P("inst"),
            P("inst", None),
            P("tp", None),
            P("tp", None),
            P("tp", None),
            P("tp", "inst"),
        ),
        out_specs=(
            P("inst", "tp", None),
            P("inst", None, "tp", None),
            P("inst", None, "tp", None),
            P("inst"),
            P(None, "inst"),
        ),
        check_vma=False,
    )
```

time: 65.9 us -> 54.6 us (0.83)
  the two profiles are of different devices: /device:TPU:6 before, /device:TPU:1 now
where the time goes in v1:
time: 54.6 us; the launch traced here: 54.4 us
  Pallas kernels  53 us (97%)
  between operations  1.45 us (3%)
    pallas_call x1, Pallas kernels, local(): pl.pallas_call(functools.partial(kernel, nz), out_shape=(jax.ShapeDtypeSt...  51.2 us
    pallas_call x1, Pallas kernels, local(): pl.pallas_call(write, out_shape=tuple((jax.ShapeDtypeStruct(a.shape, a.dt...  1.78 us

profile of v1, /device:TPU:1, one launch (start us, length us, event | category | flops | bytes accessed | tf_op | source)
XLA Modules:
  0.0 54.4 jit_solution(1405764438599398586)
XLA Ops:
  1.3 51.2 %attend.1 = (bf16[512,128]{1,0:T(8,128)(2,1)}, bf16[8,4,16,128]{3,2,1,0:T(8,128)(2,1)}, bf16[8,4,16,128]{3,2,1,0:T(8,128)(2,1)}, s32[1,64]{1,0:T(1,128)}, bf16[1,128]{1,0:T(2,128)(2,1)}) custom-call(bf16[512,128]{1,0:T(8,128)(2,1)} %bitcast.16, bf16[256,128]{1,0:T(8,128)(2,1)} %bitcast.20, bf16[256,128]{1,0:T(8,128)(2,1)} %bitcast.21, ...), custom_call_target="tpu_custom_call" | custom-call | flops 5368709120 | bytes 1048576 | tf_op jit(solution)/shard_map/attend/pallas_call | solution.py:564
  52.5 1.8 %write.1 = (bf16[512,128]{1,0:T(8,128)(2,1)}, bf16[8,4,16,128]{3,2,1,0:T(8,128)(2,1)}, bf16[8,4,16,128]{3,2,1,0:T(8,128)(2,1)}, s32[1,64]{1,0:T(1,128)}, bf16[1,128]{1,0:T(2,128)(2,1)}) custom-call(bf16[512,128]{1,0:T(8,128)(2,1)} %get-tuple-element.15.refs_0_, bf16[8,4,16,128]{3,2,1,0:T(8,128)(2,1)} %get-tuple-element.16.refs_1_, ...), custom_call_target="tpu_custom_call" | custom-call | tf_op jit(solution)/shard_map/write/pallas_call | solution.py:609

commit v2 on v1

--- a/solution.py
+++ b/solution.py
@@ -36,8 +36,8 @@
 
 NEAR, MID, FAR, LAST = (0, 1, 2), (3, 4), (5, 6), (7,)
 UNITS = (
-    (1, NEAR), (2, NEAR), (0, NEAR), (1, MID), (2, MID), (3, NEAR), (3, MID), (1, FAR), (2, FAR),
-    (3, FAR), (3, LAST), (1, LAST), (2, LAST), (0, MID), (0, FAR + LAST),
+    (0, (0,)), (1, NEAR), (2, NEAR), (0, (1, 2)), (1, MID), (2, MID), (3, NEAR), (3, MID),
+    (1, FAR), (2, FAR), (3, FAR), (3, LAST), (1, LAST), (2, LAST), (0, MID), (0, FAR + LAST),
 )
 
 
@@ -135,31 +135,23 @@
     loads[3].wait()
     pl.semaphore_wait(barrier, 6 + nz - 1)
 
-    def part(p, s):
-        if p < 2:
-            return Kb.at[s, 176:KROWS] if p else Kb.at[s, 0:176]
-        if p < 4:
-            return Vb.at[s, VROWS // 2:VROWS] if p == 3 else Vb.at[s, 0:VROWS // 2]
-        return Db.at[s]
-
     def piece(p, yy, way):
-        s = yy * 2 + c
-        return remote(part(p, s), part(p, s), sR.at[p, way, yy], rR.at[p, s], (up, down, sib)[way])
+        part = (Kb, Vb, Db)[p].at[yy * 2 + c]
+        return remote(
+            part, part, sR.at[p, way, yy], rR.at[p, yy * 2 + c], (up, down, sib)[way]
+        )
 
     def arrived(p, s):
-        remote(part(p, s), part(p, s), sR.at[p, 0, 0], rR.at[p, s], sib).wait_recv()
+        part = (Kb, Vb, Db)[p].at[s]
+        remote(part, part, sR.at[p, 0, 0], rR.at[p, s], sib).wait_recv()
 
     def qcopy(j):
         return remote(Qb.at[x], Qb.at[x], sQ.at[j], rQ.at[x], xpeer[j])
 
     span_copy = remote(svb.at[c], svb.at[c], sSV, rSV, sib)
-    def send_own(p):
-        for way in (0, 1, 2):
-            piece(p, y, way).start()
-
     span_copy.start()
-    send_own(0)
-    send_own(1)
+    for way in (0, 1, 2):
+        piece(0, y, way).start()
     qcopy(1).start()
     qcopy(2).start()
     loads[4].wait()
@@ -169,14 +161,7 @@
     half = jnp.where(c == 0, both[0:64], both[64:128])
     Vb[mine, HD:VROWS, :] = jnp.concatenate([half[0:32], half[32:64]], axis=1).astype(bf16)
 
-    def sent(p):
-        for way in (0, 1):
-            piece(p, y, way).wait_send()
-
-    sent(0)
-    send_own(2)
-    sent(1)
-    send_own(3)
+    piece(1, y, 2).start()
 
     loads[8].wait()
     dq = dq_in[...]
@@ -191,11 +176,6 @@
     mixed = nt(p_cache.astype(bf16), Vb[mine, 0:HD, :]) + nn(p_span.astype(bf16), svb[c])
     Db[mine, 0:8, :] = mixed
     Db[mine, 8:16, :] = jnp.where(iota((8, HD), 1) < HD // 2, peak, weight)
-
-    send_own(4)
-    qcopy(1).wait_send()
-    qcopy(2).wait_send()
-    qcopy(3).start()
 
     bufs = ((Sa, Pa, al_a, mn_a), (Sb, Pb, al_b, mn_b))
 
@@ -285,7 +265,7 @@
         for p in pieces:
             arrived(p, chip(k) * 2 + 1 - c)
 
-    def pass_keys(p, d):
+    def pass_keys(d, p=0):
         yu, yd = around[-d], around[d]
         arrived(p, yu * 2 + c)
         piece(p, yu, 2).start()
@@ -298,7 +278,7 @@
             if d < 3:
                 piece(p, yd, 1).start()
 
-    def pass_values(p, d):
+    def pass_values(d, p=1):
         yu, yd = around[-d], around[d]
         arrived(p, yd * 2 + c)
         piece(p, yd, 2).start()
@@ -330,6 +310,7 @@
             one = jnp.where(hit, 1.0, 0.0).astype(bf16)
             got_k.append(nn(one, Kb[s, 0:CTX, :]))
             got_v.append(nt(one, Vb[s, 0:HD, :]))
+            yield
             number = (inst(yk, x, cc) * PG + tok // PAGE + 1).astype(f32)
             found = jnp.sum(jnp.where(hit, number, 0.0), axis=1, keepdims=True) - 1.0
             here = iota((8, HD), 1) == inst(yk, x, cc)
@@ -348,8 +329,8 @@
 
     def out_copies(j):
         return (
+            remote(Ts.at[xs[j]], Tr.at[x], sT.at[j], rT.at[x], xpeer[j]),
             remote(Os.at[xs[j]], Or.at[x], sO.at[j], rO.at[x], xpeer[j]),
-            remote(Ts.at[xs[j]], Tr.at[x], sT.at[j], rT.at[x], xpeer[j]),
         )
 
     def send_out(j):
@@ -364,7 +345,7 @@
 
     def decode_column():
         for k in range(8):
-            arrived(4, chip(k) * 2 + 1 - c)
+            arrived(2, chip(k) * 2 + 1 - c)
         o, peak, weight = merge(Db[...])
         DX[x, 0:8, :] = o
         DX[x, 8:16, :] = jnp.where(iota((8, HD), 1) < HD // 2, peak, weight)
@@ -395,72 +376,74 @@
         remote(Qb.at[xs[j]], Qb.at[xs[j]], sQ.at[j], rQ.at[xs[j]], xpeer[j]).wait_recv()
 
     def before(f):
-        if f == 0:
-            pass_values(2, 1)
-            pass_values(3, 1)
         if f == 1:
-            for k in (0, 1, 2):
-                wait_chip((2, 3), k)
-        if f in (2, 4, 7):
-            pass_keys(0, f // 2 + 1 if f < 7 else 4)
-            pass_keys(1, f // 2 + 1 if f < 7 else 4)
+            pass_values(1)
         if f == 2:
-            for k in (0, 1, 2):
-                pages(k)
+            for k in (1, 2):
+                wait_chip((1,), k)
+        if f in (3, 5, 8):
+            pass_keys({3: 2, 5: 3, 8: 4}[f])
+        if f in (3, 6, 9):
+            pass_values(f // 3 + 1)
+        if f in (3, 6, 9, 11):
+            pass_values({3: 1, 6: 2, 9: 3, 11: 4}[f], 2)
+        if f == 3:
             for k in (3, 4):
-                wait_chip((0, 1), k)
-        if f in (3, 6, 9):
-            pass_values(2, f // 3 + 1)
-            pass_values(3, f // 3 + 1)
-        if f in (2, 5, 8, 10):
-            pass_values(4, {2: 1, 5: 2, 8: 3, 10: 4}[f])
-        if f == 4:
+                wait_chip((0,), k)
+        if f == 5:
             arrived_query(3)
             for k in (3, 4):
-                wait_chip((2, 3), k)
-        if f == 5:
-            pages(3)
-            pages(4)
-        if f == 6:
+                wait_chip((1,), k)
+        if f == 7:
             for k in (5, 6):
-                wait_chip((0, 1), k)
-        if f == 8:
+                wait_chip((0,), k)
+        if f == 9:
             for k in (5, 6):
-                wait_chip((2, 3), k)
-        if f == 9:
-            wait_chip((0, 1), 7)
+                wait_chip((1,), k)
         if f == 10:
-            pages(5)
-            pages(6)
-        if f == 11:
-            wait_chip((2, 3), 7)
+            wait_chip((0,), 7)
+        if f == 12:
+            wait_chip((1,), 7)
+        if f == 13:
+            send_out(3)
+        if f == 14:
+            send_out(1)
+        if f == 15:
+            send_out(2)
+            send_ids()
             decode_column()
-        if f == 12:
-            send_out(3)
-            pages(7)
-            send_ids()
-        if f == 13:
-            send_out(1)
-        if f == 14:
-            send_out(2)
-            decode_project()
-
-    pass_keys(0, 1)
-    pass_keys(1, 1)
+
+    wait_chip((0,), 0)
+    together(scores(0))
+    for p in (1, 2):
+        if p == 1:
+            for way in (0, 1):
+                piece(0, y, way).wait_send()
+        for way in (0, 1, 2):
+            if p == 2 or way < 2:
+                piece(p, y, way).start()
+    wait_chip((1,), 0)
+    together(weights(0), pages(0))
+    qcopy(1).wait_send()
+    qcopy(2).wait_send()
+    qcopy(3).start()
+    pass_keys(1)
     arrived_query(1)
-    for k in (0, 1, 2):
-        wait_chip((0, 1), k)
-    together(scores(0))
+    for k in (1, 2):
+        wait_chip((0,), k)
+    together(values(0), scores(1))
     arrived_query(2)
     end = len(UNITS)
-    for f in range(end):
+    beside = {3: (1, 2), 6: (3, 4), 10: (5, 6), 14: (7,)}
+    for f in range(1, end):
         before(f)
-        stages = [values(f - 1)] if f else []
+        stages = [values(f - 1)] if f > 1 else []
         stages.append(weights(f))
         if f + 1 < end:
             stages.append(scores(f + 1))
-        together(*stages)
+        together(*stages, *(pages(k) for k in beside.get(f, ())))
     together(values(end - 1))
+    decode_project()
 
     for j in (1, 2, 3):
         v = xs[j]
@@ -491,10 +474,30 @@
     stores.append(pltpu.make_async_copy(dec_stage, dec_out, lsem.at[22]))
     stores[-1].start()
 
+    for p in range(3):
+        for d in range(4):
+            if d == 0 and p == 0:
+                continue
+            if p == 0 or d < 3:
+                piece(p, around[-d], 0).wait_send()
+            if p > 0 or d < 3:
+                piece(p, around[d], 1).wait_send()
+        for yy in range(NY):
+            piece(p, yy, 2).wait_send()
+    span_copy.wait_send()
+    qcopy(3).wait_send()
+    for j in (1, 2, 3):
+        for yk in range(NY):
+            page_copy(j, yk).wait_send()
+        remote(Is.at[xs[j]], Ir.at[x], sI.at[j], rI.at[x], xpeer[j]).wait_send()
+        remote(DX.at[x], DX.at[x], sX.at[j], rX.at[x], xpeer[j]).wait_send()
+    for j, zz in enumerate(zpeers):
+        remote(Zb.at[z], Zb.at[z], sZ.at[j], rZ.at[z], me, zz).wait_send()
+
     for j in (1, 2, 3):
         v = xs[j]
-        remote(Os.at[v], Or.at[v], sO.at[j], rO.at[v], xpeer[j]).wait_recv()
         remote(Ts.at[v], Tr.at[v], sT.at[j], rT.at[v], xpeer[j]).wait_recv()
+
     def stat(j, first):
         return jnp.concatenate(
             [Tr[xs[j], first + t:first + t + 1, :] for t in range(R // HD)], axis=1
@@ -508,33 +511,16 @@
     shares = [w / whole for w in shares]
     mix = acc[x] * shares[0]
     for j in (1, 2, 3):
-        mix = mix + Or[xs[j]].astype(f32) * shares[j]
+        v = xs[j]
+        remote(Os.at[v], Or.at[v], sO.at[j], rO.at[v], xpeer[j]).wait_recv()
+        mix = mix + Or[v].astype(f32) * shares[j]
     ostage[...] = mix.T.astype(bf16)
     done = pltpu.make_async_copy(ostage, out, lsem.at[7])
     done.start()
 
-    for p in range(5):
-        for d in range(4):
-            if d == 0 and p < 2:
-                continue
-            if p < 2 or d < 3:
-                piece(p, around[-d], 0).wait_send()
-            if p > 1 or d < 3:
-                piece(p, around[d], 1).wait_send()
-        for yy in range(NY):
-            piece(p, yy, 2).wait_send()
-    span_copy.wait_send()
     for j in (1, 2, 3):
-        if j == 3:
-            qcopy(j).wait_send()
         for copy in out_copies(j):
             copy.wait_send()
-        for yk in range(NY):
-            page_copy(j, yk).wait_send()
-        remote(Is.at[xs[j]], Ir.at[x], sI.at[j], rI.at[x], xpeer[j]).wait_send()
-        remote(DX.at[x], DX.at[x], sX.at[j], rX.at[x], xpeer[j]).wait_send()
-    for j, zz in enumerate(zpeers):
-        remote(Zb.at[z], Zb.at[z], sZ.at[j], rZ.at[z], me, zz).wait_send()
     for store in stores:
         store.wait()
     done.wait()
@@ -586,7 +572,7 @@
             V((NX, 8, HD), i32), V((NX, 8, HD), i32),
             V((NX, 16, HD), f32), V((nz, 8, HD), f32), V((R, HD), bf16),
             D((23,)),
-            D((5, 3, NY)), D((5, 2 * NY)),
+            D((3, 3, NY)), D((3, 2 * NY)),
             D, D,
             D((NX,)), D((NX,)), D((NX,)), D((NX,)), D((NX,)), D((NX,)), D((NX, NY)), D((NX, NY)),
             D((NX,)), D((NX,)), D((NX,)), D((NX,)),

time: 54.6 us -> 58 us (1.062); the launches traced: 54.4 us -> 57 us
  Pallas kernels: 53 us -> 55.5 us
    pallas_call x1, Pallas kernels: 51.2 us -> 53.7 us  [local(): pl.pallas_call(functools.partial(kernel, nz), out_shape=(jax.ShapeDtypeSt...]
where the time goes in v2:
time: 58 us; the launch traced here: 57 us
  Pallas kernels  55.5 us (96%)
  between operations  1.45 us (2%)
    pallas_call x1, Pallas kernels, local(): pl.pallas_call(functools.partial(kernel, nz), out_shape=(jax.ShapeDtypeSt...  53.7 us
    pallas_call x1, Pallas kernels, local(): pl.pallas_call(write, out_shape=tuple((jax.ShapeDtypeStruct(a.shape, a.dt...  1.78 us

profile of v2, /device:TPU:1, one launch (start us, length us, event | category | flops | bytes accessed | tf_op | source)
XLA Modules:
  0.0 57.0 jit_solution(12223577231863735277)
XLA Ops:
  1.3 53.7 %attend.1 = (bf16[512,128]{1,0:T(8,128)(2,1)}, bf16[8,4,16,128]{3,2,1,0:T(8,128)(2,1)}, bf16[8,4,16,128]{3,2,1,0:T(8,128)(2,1)}, s32[1,64]{1,0:T(1,128)}, bf16[1,128]{1,0:T(2,128)(2,1)}) custom-call(bf16[512,128]{1,0:T(8,128)(2,1)} %bitcast.16, bf16[256,128]{1,0:T(8,128)(2,1)} %bitcast.20, bf16[256,128]{1,0:T(8,128)(2,1)} %bitcast.21, ...), custom_call_target="tpu_custom_call" | custom-call | flops 5368709120 | bytes 1048576 | tf_op jit(solution)/shard_map/attend/pallas_call | solution.py:550
  55.0 1.8 %write.1 = (bf16[512,128]{1,0:T(8,128)(2,1)}, bf16[8,4,16,128]{3,2,1,0:T(8,128)(2,1)}, bf16[8,4,16,128]{3,2,1,0:T(8,128)(2,1)}, s32[1,64]{1,0:T(1,128)}, bf16[1,128]{1,0:T(2,128)(2,1)}) custom-call(bf16[512,128]{1,0:T(8,128)(2,1)} %get-tuple-element.15.refs_0_, bf16[8,4,16,128]{3,2,1,0:T(8,128)(2,1)} %get-tuple-element.16.refs_1_, ...), custom_call_target="tpu_custom_call" | custom-call | tf_op jit(solution)/shard_map/write/pallas_call | solution.py:595

commit v3 on v2

--- a/solution.py
+++ b/solution.py
@@ -406,12 +406,13 @@
             wait_chip((1,), 7)
         if f == 13:
             send_out(3)
+            decode_column()
         if f == 14:
             send_out(1)
         if f == 15:
             send_out(2)
             send_ids()
-            decode_column()
+            decode_project()
 
     wait_chip((0,), 0)
     together(scores(0))
@@ -443,7 +444,6 @@
             stages.append(scores(f + 1))
         together(*stages, *(pages(k) for k in beside.get(f, ())))
     together(values(end - 1))
-    decode_project()
 
     for j in (1, 2, 3):
         v = xs[j]
@@ -465,15 +465,6 @@
     stores.append(pltpu.make_async_copy(held_stage, ids_out, lsem.at[21]))
     stores[-1].start()
 
-    for j, zz in enumerate(zpeers):
-        remote(Zb.at[zz], Zb.at[zz], sZ.at[j], rZ.at[zz], me, zz).wait_recv()
-    total = Zb[0]
-    for v in range(1, nz):
-        total = total + Zb[v]
-    dec_stage[...] = jnp.sum(total, axis=0, keepdims=True).astype(bf16)
-    stores.append(pltpu.make_async_copy(dec_stage, dec_out, lsem.at[22]))
-    stores[-1].start()
-
     for p in range(3):
         for d in range(4):
             if d == 0 and p == 0:
@@ -517,6 +508,15 @@
     ostage[...] = mix.T.astype(bf16)
     done = pltpu.make_async_copy(ostage, out, lsem.at[7])
     done.start()
+
+    for j, zz in enumerate(zpeers):
+        remote(Zb.at[zz], Zb.at[zz], sZ.at[j], rZ.at[zz], me, zz).wait_recv()
+    total = Zb[0]
+    for v in range(1, nz):
+        total = total + Zb[v]
+    dec_stage[...] = jnp.sum(total, axis=0, keepdims=True).astype(bf16)
+    stores.append(pltpu.make_async_copy(dec_stage, dec_out, lsem.at[22]))
+    stores[-1].start()
 
     for j in (1, 2, 3):
         for copy in out_copies(j):

time: 58 us -> 54.9 us (0.947)
  the two profiles are of different devices: /device:TPU:1 before, /device:TPU:10 now
where the time goes in v3:
time: 54.9 us; the launch traced here: 54.7 us
  Pallas kernels  53.3 us (97%)
  between operations  1.45 us (3%)
    pallas_call x1, Pallas kernels, local(): pl.pallas_call(functools.partial(kernel, nz), out_shape=(jax.ShapeDtypeSt...  51.5 us
    pallas_call x1, Pallas kernels, local(): pl.pallas_call(write, out_shape=tuple((jax.ShapeDtypeStruct(a.shape, a.dt...  1.78 us

profile of v3, /device:TPU:10, one launch (start us, length us, event | category | flops | bytes accessed | tf_op | source)
XLA Modules:
  0.0 54.7 jit_solution(2958394070339413021)
XLA Ops:
  1.3 51.5 %attend.1 = (bf16[512,128]{1,0:T(8,128)(2,1)}, bf16[8,4,16,128]{3,2,1,0:T(8,128)(2,1)}, bf16[8,4,16,128]{3,2,1,0:T(8,128)(2,1)}, s32[1,64]{1,0:T(1,128)}, bf16[1,128]{1,0:T(2,128)(2,1)}) custom-call(bf16[512,128]{1,0:T(8,128)(2,1)} %bitcast.16, bf16[256,128]{1,0:T(8,128)(2,1)} %bitcast.20, bf16[256,128]{1,0:T(8,128)(2,1)} %bitcast.21, ...), custom_call_target="tpu_custom_call" | custom-call | flops 5368709120 | bytes 1048576 | tf_op jit(solution)/shard_map/attend/pallas_call | solution.py:550
  52.8 1.8 %write.1 = (bf16[512,128]{1,0:T(8,128)(2,1)}, bf16[8,4,16,128]{3,2,1,0:T(8,128)(2,1)}, bf16[8,4,16,128]{3,2,1,0:T(8,128)(2,1)}, s32[1,64]{1,0:T(1,128)}, bf16[1,128]{1,0:T(2,128)(2,1)}) custom-call(bf16[512,128]{1,0:T(8,128)(2,1)} %get-tuple-element.15.refs_0_, bf16[8,4,16,128]{3,2,1,0:T(8,128)(2,1)} %get-tuple-element.16.refs_1_, ...), custom_call_target="tpu_custom_call" | custom-call | tf_op jit(solution)/shard_map/write/pallas_call | solution.py:595
